TPU v7x, 32 devices: a whole 2x2x4 slice. The times are simulated.
32 devices in a mesh: grid: 4 (over z), patch: 4 (over y, x), cross: 2 (over core).
Axes of the slice: x: 2, y: 2, z: 4, core: 2. Of those that a mesh axis runs over, the one named last changes fastest.
Arguments:
- adjoint_now: float32 [3, 4, 32, 16, 128], P(None, 'grid', 'patch', 'cross'), may hold values from -6 to 6
- adjoint_prev: float32 [3, 4, 32, 16, 128], P(None, 'grid', 'patch', 'cross'), may hold values from -6 to 6
- stiffness: float32 [4, 32, 16, 128], P('grid', 'patch', 'cross'), may hold values from 0.08 to 0.3
- adjoint_source: bfloat16 [2, 3, 4, 32, 16, 128], P(None, None, 'grid', 'patch', 'cross'), may hold values from -6 to 6
- forward_field: bfloat16 [2, 3, 4, 32, 16, 128], P(None, None, 'grid', 'patch', 'cross'), may hold values from -6 to 6
- material_mask: int32 [4, 4, 2], P('grid', 'patch', 'cross'), may hold values 0 or 1
- interface_map: int32 [4, 32, 16], P('grid', 'patch', 'cross'), may hold values from 0 to 63, as said below
Outputs:
- adjoint_final: float32 [3, 4, 32, 16, 128], P(None, 'grid', 'patch', 'cross')
- kernel: float32 [4, 32, 16, 128], P('grid', 'patch', 'cross')
Inputs may be any that keep to these rules, and one draw needn't show every extreme that they name: `interface_map`: each value indexes a column of the same patch's plane of 8 x 8 cells, row-major, at most one cell away from the cell's own position along each horizontal dimension; the first and last cells of each patch are fed by their own column.
All inputs are finite; a program needn't handle non-finite values. No bound on the sum of `material_mask` on one device may be relied on, other than what follows from the above.
Results may differ from a plain program's by a relative error of at most 0.00035.
Values sent between devices are 32-bit elements; how exact they have to be, the bound alone decides.
A program may use at most 64 MiB of HBM per device.

v0:
```python
import jax
import jax.numpy as jnp
from jax import lax
from jax.sharding import PartitionSpec as P

STEPS = 2


def with_halo(value, sides, width):
    for axis, dim in sides:
        peers, length = (lax.axis_size(axis), value.shape[dim])
        up = [(i, (i + 1) % peers) for i in range(peers)]
        down = [(j, i) for i, j in up]
        last = lax.slice_in_dim(value, length - width, length, axis=dim)
        initial = lax.slice_in_dim(value, 0, width, axis=dim)
        before = lax.ppermute(last, axis, up)
        after = lax.ppermute(initial, axis, down)
        value = jnp.concatenate([before, value, after], axis=dim)
    return value


def shifted(value, axis, by):
    peers = lax.axis_size(axis)
    pairs = [(i, i + by) for i in range(peers) if 0 <= i + by < peers]
    return lax.ppermute(value, axis, pairs)


def side_sums(field):
    padded = with_halo(field, (("patch", 2), ("cross", 3)), 1)
    total = padded[:, :, 2:, 1:-1] + padded[:, :, :-2, 1:-1]
    total = total + padded[:, :, 1:-1, 2:] + padded[:, :, 1:-1, :-2]
    return total


def local(
    adjoint_now,
    adjoint_prev,
    stiffness,
    adjoint_source,
    forward_field,
    material_mask,
    interface_map,
):
    rows = adjoint_now.shape[2]
    cols = adjoint_now.shape[3]
    flat_map = interface_map.reshape(-1)
    is_top = lax.axis_index("grid") == 0
    patch_mask = material_mask[0, 0, 0].astype(jnp.float32)
    field = adjoint_now
    older = adjoint_prev
    kernel = jnp.zeros(stiffness.shape, jnp.float32)
    for step in range(STEPS):
        slot = STEPS - 1 - step
        bottom = field[:, :, :, :, -1]
        from_above = shifted(bottom, "grid", 1)
        from_below = shifted(field[:, :, :, :, 0], "grid", -1)
        gathered = jnp.take(from_above.reshape(3, rows * cols), flat_map, axis=1).reshape(
            3, 1, rows, cols
        )
        top_plane = jnp.where(is_top, field[:, :, :, :, 0], gathered)
        upper = jnp.concatenate([top_plane[..., None], field[..., :-1]], axis=4)
        lower = jnp.concatenate([field[..., 1:], from_below[..., None]], axis=4)
        lap = side_sums(field) + upper + lower - 6.0 * field
        fresh = (
            2.0 * field - older + stiffness * lap + adjoint_source[slot].astype(jnp.float32)
        ) * patch_mask
        kernel = kernel + jnp.sum(fresh * forward_field[slot].astype(jnp.float32), axis=0)
        older = field
        field = fresh
    return (field, kernel)


def solution(mesh):
    in_specs = (
        P(None, "grid", "patch", "cross", None),
        P(None, "grid", "patch", "cross", None),
        P("grid", "patch", "cross", None),
        P(None, None, "grid", "patch", "cross", None),
        P(None, None, "grid", "patch", "cross", None),
        P("grid", "patch", "cross"),
        P("grid", "patch", "cross"),
    )
    out_specs = (P(None, "grid", "patch", "cross", None), P("grid", "patch", "cross", None))
    return jax.shard_map(local, mesh=mesh, in_specs=in_specs, out_specs=out_specs, check_vma=False)
```

profile of v0, /device:TPU:0, one launch (start us, length us, event | category | flops | bytes accessed | tf_op | source)
XLA Modules:
  0.0 35.0 jit_solution(15187314127477601255)
XLA Ops:
  0.6 0.7 %fusion.27 = (f32[3,1,1,8,128]{4,3,2,1,0:T(8,128)S(1)}, f32[3,1,1,8,128]{4,3,2,1,0:T(8,128)S(1)}) fusion(f32[3,1,8,8,128]{4,3,2,1,0:T(8,128)} %param.9), kind=kLoop, calls=%fused_computation.63 | loop fusion | bytes 49152 | tf_op jit(solution)/shard_map/slice | solution.py:15
  1.4 3.9 %collective-permute-start = (f32[3,1,1,8,128]{4,3,2,1,0:T(8,128)S(1)}, f32[3,1,1,8,128]{4,3,2,1,0:T(8,128)S(1)}, u32[]{:S(2)}, u32[]{:S(2)}) collective-permute-start(f32[3,1,1,8,128]{4,3,2,1,0:T(8,128)S(1)} %get-tuple-element.30), channel_id=1, source_target_pairs={{2,0},{4,2},{6,4},{0,6},{3,1},{5,3},{7,5},{1,7},{10,8},{12,10},{14... | collective-permute-start | bytes 36872 | tf_op jit(solution)/shard_map/ppermute | solution.py:17
  5.3 1.0 %slice.103 = f32[3,1,8,8,1]{4,3,2,1,0:T(8,128)S(1)} slice(f32[3,1,8,8,128]{4,3,2,1,0:T(8,128)} %param.9), slice={[0:3], [0:1], [0:8], [0:8], [127:128]} | slice | bytes 1536 | tf_op jit(solution)/shard_map/slice | solution.py:54
  6.5 3.5 %collective-permute-start.4 = (f32[3,1,8,8]{3,2,0,1:T(8,128)S(1)}, f32[3,1,8,8]{3,2,0,1:T(8,128)S(1)}, u32[]{:S(2)}, u32[]{:S(2)}) collective-permute-start(f32[3,1,8,8]{3,2,0,1:T(8,128)S(1)} %bitcast.55), channel_id=1, source_target_pairs={{0,8},{8,16},{16,24},{1,9},{9,17},{17,25},{2,10},{10,18},{18,26},{... | collective-permute-start | bytes 2312 | tf_op jit(solution)/shard_map/ppermute | solution.py:25
  10.1 1.3 %collective-permute-done.4 = f32[3,1,8,8]{3,2,0,1:T(8,128)S(1)} collective-permute-done((f32[3,1,8,8]{3,2,0,1:T(8,128)S(1)}, f32[3,1,8,8]{3,2,0,1:T(8,128)S(1)}, u32[]{:S(2)}, u32[]{:S(2)}) %collective-permute-start.4) | collective-permute-done | bytes 800 | tf_op jit(solution)/shard_map/ppermute | solution.py:25
  11.5 0.6 %gather_fusion = f32[64,3]{1,0:T(8,128)S(1)} fusion(f32[3,64]{0,1:T(8,128)S(1)} %bitcast.49, s32[1024]{0:T(1024)S(1)} %pad_clamp_fusion), kind=kCustom, calls=%fused_computation.clone | custom fusion | bytes 1792 | tf_op jit(solution)/shard_map/jit(_take)/gather | solution.py:57
  12.1 0.5 %copy.165 = f32[3,1,8,8,1]{4,3,2,1,0:T(8,128)S(1)} copy(f32[3,1,8,8,1]{0,3,2,4,1:T(8,128)S(1)} %select_bitcast_fusion.1) | data formatting | bytes 1536 | tf_op jit(solution)/shard_map/reshape | solution.py:57
  12.7 0.3 copy-done
  13.0 1.3 %collective-permute-start.5 = (f32[3,1,8,8]{3,2,0,1:T(8,128)S(1)}, f32[3,1,8,8]{3,2,0,1:T(8,128)S(1)}, u32[]{:S(2)}, u32[]{:S(2)}) collective-permute-start(f32[3,1,8,8]{3,2,0,1:T(8,128)S(1)} %bitcast.50), channel_id=1, source_target_pairs={{8,0},{16,8},{24,16},{9,1},{17,9},{25,17},{10,2},{18,10},{26,18},{... | collective-permute-start | bytes 2312 | tf_op jit(solution)/shard_map/ppermute | solution.py:25
  14.5 0.5 %collective-permute-start.3 = (f32[3,1,10,1,128]{4,3,2,1,0:T(1,128)S(1)}, f32[3,1,10,1,128]{4,3,2,1,0:T(1,128)S(1)}, u32[]{:S(2)}, u32[]{:S(2)}) collective-permute-start(f32[3,1,10,1,128]{4,3,2,1,0:T(1,128)S(1)} %get-tuple-element.21), channel_id=1, source_target_pairs={{0,1},{1,0},{2,3},{3,2},{4,5},{5,4},{6,7},{7,6},{8,9},{9,8},{10,11... | collective-permute-start | bytes 46088 | tf_op jit(solution)/shard_map/ppermute | solution.py:16
  15.8 3.1 %collective-permute-done.5 = f32[3,1,8,8]{3,2,0,1:T(8,128)S(1)} collective-permute-done((f32[3,1,8,8]{3,2,0,1:T(8,128)S(1)}, f32[3,1,8,8]{3,2,0,1:T(8,128)S(1)}, u32[]{:S(2)}, u32[]{:S(2)}) %collective-permute-start.5) | collective-permute-done | bytes 800 | tf_op jit(solution)/shard_map/ppermute | solution.py:25
  19.1 0.5 %copy-done.1 = f32[1,8,8,128]{3,2,1,0:T(8,128)S(1)} copy-done((f32[1,8,8,128]{3,2,1,0:T(8,128)S(1)}, f32[1,8,8,128]{3,2,1,0:T(8,128)}, u32[]{:S(2)}) %copy-start.1) | copy-done | bytes 32792
  20.1 3.9 %collective-permute-start.10 = (f32[3,1,8,8]{3,2,0,1:T(8,128)S(1)}, f32[3,1,8,8]{3,2,0,1:T(8,128)S(1)}, u32[]{:S(2)}, u32[]{:S(2)}) collective-permute-start(f32[3,1,8,8]{3,2,0,1:T(8,128)S(1)} %bitcast.54), channel_id=1, source_target_pairs={{0,8},{8,16},{16,24},{1,9},{9,17},{17,25},{2,10},{10,18},{18,26},{... | collective-permute-start | bytes 2312 | tf_op jit(solution)/shard_map/ppermute | solution.py:25
  24.0 2.0 %collective-permute-start.7 = (f32[3,1,1,8,128]{4,3,2,1,0:T(8,128)S(1)}, f32[3,1,1,8,128]{4,3,2,1,0:T(8,128)S(1)}, u32[]{:S(2)}, u32[]{:S(2)}) collective-permute-start(f32[3,1,1,8,128]{4,3,2,1,0:T(8,128)S(1)} %get-tuple-element.22), channel_id=1, source_target_pairs={{0,2},{2,4},{4,6},{6,0},{1,3},{3,5},{5,7},{7,1},{8,10},{10,12},{12... | collective-permute-start | bytes 36872 | tf_op jit(solution)/shard_map/ppermute | solution.py:16
  26.0 1.0 %collective-permute-start.6 = (f32[3,1,1,8,128]{4,3,2,1,0:T(8,128)S(1)}, f32[3,1,1,8,128]{4,3,2,1,0:T(8,128)S(1)}, u32[]{:S(2)}, u32[]{:S(2)}) collective-permute-start(f32[3,1,1,8,128]{4,3,2,1,0:T(8,128)S(1)} %get-tuple-element.23), channel_id=1, source_target_pairs={{2,0},{4,2},{6,4},{0,6},{3,1},{5,3},{7,5},{1,7},{10,8},{12,10},{14... | collective-permute-start | bytes 36872 | tf_op jit(solution)/shard_map/ppermute | solution.py:17
  27.1 1.3 %collective-permute-start.11 = (f32[3,1,8,8]{3,2,0,1:T(8,128)S(1)}, f32[3,1,8,8]{3,2,0,1:T(8,128)S(1)}, u32[]{:S(2)}, u32[]{:S(2)}) collective-permute-start(f32[3,1,8,8]{3,2,0,1:T(8,128)S(1)} %bitcast.51), channel_id=1, source_target_pairs={{8,0},{16,8},{24,16},{9,1},{17,9},{25,17},{10,2},{18,10},{26,18},{... | collective-permute-start | bytes 2312 | tf_op jit(solution)/shard_map/ppermute | solution.py:25
  28.5 0.6 %gather_fusion.1 = f32[64,3]{1,0:T(8,128)S(1)} fusion(f32[3,64]{0,1:T(8,128)S(1)} %bitcast.48, s32[1024]{0:T(1024)S(1)} %pad_clamp_fusion), kind=kCustom, calls=%fused_computation.1.clone | custom fusion | bytes 1792 | tf_op jit(solution)/shard_map/jit(_take)/gather | solution.py:57
  29.2 0.5 %copy.170 = f32[3,1,8,8,1]{4,3,2,1,0:T(8,128)S(1)} copy(f32[3,1,8,8,1]{0,3,2,4,1:T(8,128)S(1)} %select_bitcast_fusion) | data formatting | bytes 1536 | tf_op jit(solution)/shard_map/reshape | solution.py:57
  29.8 0.5 %collective-permute-start.9 = (f32[3,1,10,1,128]{4,3,2,1,0:T(1,128)S(1)}, f32[3,1,10,1,128]{4,3,2,1,0:T(1,128)S(1)}, u32[]{:S(2)}, u32[]{:S(2)}) collective-permute-start(f32[3,1,10,1,128]{4,3,2,1,0:T(1,128)S(1)} %get-tuple-element.19), channel_id=1, source_target_pairs={{0,1},{1,0},{2,3},{3,2},{4,5},{5,4},{6,7},{7,6},{8,9},{9,8},{10,11... | collective-permute-start | bytes 46088 | tf_op jit(solution)/shard_map/ppermute | solution.py:16
  30.4 2.3 %collective-permute-done.11 = f32[3,1,8,8]{3,2,0,1:T(8,128)S(1)} collective-permute-done((f32[3,1,8,8]{3,2,0,1:T(8,128)S(1)}, f32[3,1,8,8]{3,2,0,1:T(8,128)S(1)}, u32[]{:S(2)}, u32[]{:S(2)}) %collective-permute-start.11) | collective-permute-done | bytes 800 | tf_op jit(solution)/shard_map/ppermute | solution.py:25
  32.9 0.8 %fusion.20 = (f32[8,8,128]{2,1,0:T(8,128)S(1)}, f32[8,8,128]{2,1,0:T(8,128)S(1)}, f32[3,1,8,8,128]{4,3,2,1,0:T(8,128)}) fusion(bf16[2,3,1,8,8,128]{5,4,3,1,2,0:T(8,128)(2,1)S(1)} %bitcast.47, f32[3,1,8,8,128]{4,3,2,1,0:T(8,128)S(1)} %fusion.17, f32[]{:T(128)} %bitcast.8, bf16[2,3,1,8,8,128]{5,4,3,1,2,0:T(8,128)(2,1)S(1)} %bitcast.46, ...), kind=kLoop, calls=%fused_computation.37 | loop fusion | flops 720896 | bytes 792580 | tf_op jit(solution)/shard_map/reduce_sum | solution.py:67
  33.7 0.2 copy.183
  33.9 0.2 copy.182
  34.2 0.8 %copy.177 = f32[1,8,8,128]{3,2,1,0:T(8,128)} copy(f32[1,8,8,128]{2,1,3,0:T(8,128)S(1)} %add_bitcast_fusion) | data formatting | bytes 65536
  (46 shorter events, 2.1 us)
Async XLA Ops:
  1.4 13.0 %collective-permute-start = (f32[3,1,1,8,128]{4,3,2,1,0:T(8,128)S(1)}, f32[3,1,1,8,128]{4,3,2,1,0:T(8,128)S(1)}, u32[]{:S(2)}, u32[]{:S(2)}) collective-permute-start(f32[3,1,1,8,128]{4,3,2,1,0:T(8,128)S(1)} %get-tuple-element.30), channel_id=1, source_target_pairs={{2,0},{4,2},{6,4},{0,6},{3,1},{5,3},{7,5},{1,7},{10,8},{12,10},{14... | collective-permute-start | bytes 36872 | tf_op jit(solution)/shard_map/ppermute | solution.py:17
  5.3 9.1 %collective-permute-start.1 = (f32[3,1,1,8,128]{4,3,2,1,0:T(8,128)S(1)}, f32[3,1,1,8,128]{4,3,2,1,0:T(8,128)S(1)}, u32[]{:S(2)}, u32[]{:S(2)}) collective-permute-start(f32[3,1,1,8,128]{4,3,2,1,0:T(8,128)S(1)} %get-tuple-element.31), channel_id=1, source_target_pairs={{0,2},{2,4},{4,6},{6,0},{1,3},{3,5},{5,7},{7,1},{8,10},{10,12},{12... | collective-permute-start | bytes 36872 | tf_op jit(solution)/shard_map/ppermute | solution.py:16
  6.2 3.7 %copy-start.5 = (s32[1,8,8]{2,1,0:T(8,128)S(1)}, s32[1,8,8]{2,1,0:T(8,128)}, u32[]{:S(2)}) copy-start(s32[1,8,8]{2,1,0:T(8,128)} %param.15) | copy-start | bytes 772
  6.5 4.9 %collective-permute-start.4 = (f32[3,1,8,8]{3,2,0,1:T(8,128)S(1)}, f32[3,1,8,8]{3,2,0,1:T(8,128)S(1)}, u32[]{:S(2)}, u32[]{:S(2)}) collective-permute-start(f32[3,1,8,8]{3,2,0,1:T(8,128)S(1)} %bitcast.55), channel_id=1, source_target_pairs={{0,8},{8,16},{16,24},{1,9},{9,17},{17,25},{2,10},{10,18},{18,26},{... | collective-permute-start | bytes 2312 | tf_op jit(solution)/shard_map/ppermute | solution.py:25
  12.0 0.9 %copy-start = (f32[3,1,8,8,128]{4,3,2,1,0:T(8,128)S(1)}, f32[3,1,8,8,128]{4,3,2,1,0:T(8,128)}, u32[]{:S(2)}) copy-start(f32[3,1,8,8,128]{4,3,2,1,0:T(8,128)} %param.9) | copy-start | bytes 294916
  13.0 5.9 %collective-permute-start.5 = (f32[3,1,8,8]{3,2,0,1:T(8,128)S(1)}, f32[3,1,8,8]{3,2,0,1:T(8,128)S(1)}, u32[]{:S(2)}, u32[]{:S(2)}) collective-permute-start(f32[3,1,8,8]{3,2,0,1:T(8,128)S(1)} %bitcast.50), channel_id=1, source_target_pairs={{8,0},{16,8},{24,16},{9,1},{17,9},{25,17},{10,2},{18,10},{26,18},{... | collective-permute-start | bytes 2312 | tf_op jit(solution)/shard_map/ppermute | solution.py:25
  14.4 4.7 %collective-permute-start.2 = (f32[3,1,10,1,128]{4,3,2,1,0:T(1,128)S(1)}, f32[3,1,10,1,128]{4,3,2,1,0:T(1,128)S(1)}, u32[]{:S(2)}, u32[]{:S(2)}) collective-permute-start(f32[3,1,10,1,128]{4,3,2,1,0:T(1,128)S(1)} %get-tuple-element.20), channel_id=1, source_target_pairs={{1,0},{0,1},{3,2},{2,3},{5,4},{4,5},{7,6},{6,7},{9,8},{8,9},{11,10... | collective-permute-start | bytes 46088 | tf_op jit(solution)/shard_map/ppermute | solution.py:17
  14.5 4.6 %collective-permute-start.3 = (f32[3,1,10,1,128]{4,3,2,1,0:T(1,128)S(1)}, f32[3,1,10,1,128]{4,3,2,1,0:T(1,128)S(1)}, u32[]{:S(2)}, u32[]{:S(2)}) collective-permute-start(f32[3,1,10,1,128]{4,3,2,1,0:T(1,128)S(1)} %get-tuple-element.21), channel_id=1, source_target_pairs={{0,1},{1,0},{2,3},{3,2},{4,5},{5,4},{6,7},{7,6},{8,9},{9,8},{10,11... | collective-permute-start | bytes 46088 | tf_op jit(solution)/shard_map/ppermute | solution.py:16
  15.0 4.1 %copy-start.2 = (bf16[2,3,1,8,8,128]{5,4,3,2,1,0:T(8,128)(2,1)S(1)}, bf16[2,3,1,8,8,128]{5,4,3,2,1,0:T(8,128)(2,1)}, u32[]{:S(2)}) copy-start(bf16[2,3,1,8,8,128]{5,4,3,2,1,0:T(8,128)(2,1)} %param.12) | copy-start | bytes 294916
  15.0 4.1 %copy-start.3 = (f32[3,1,8,8,128]{4,3,2,1,0:T(8,128)S(1)}, f32[3,1,8,8,128]{4,3,2,1,0:T(8,128)}, u32[]{:S(2)}) copy-start(f32[3,1,8,8,128]{4,3,2,1,0:T(8,128)} %param.10) | copy-start | bytes 294916
  18.9 0.8 %copy-start.1 = (f32[1,8,8,128]{3,2,1,0:T(8,128)S(1)}, f32[1,8,8,128]{3,2,1,0:T(8,128)}, u32[]{:S(2)}) copy-start(f32[1,8,8,128]{3,2,1,0:T(8,128)} %param.11) | copy-start | bytes 98308
  20.1 8.3 %collective-permute-start.10 = (f32[3,1,8,8]{3,2,0,1:T(8,128)S(1)}, f32[3,1,8,8]{3,2,0,1:T(8,128)S(1)}, u32[]{:S(2)}, u32[]{:S(2)}) collective-permute-start(f32[3,1,8,8]{3,2,0,1:T(8,128)S(1)} %bitcast.54), channel_id=1, source_target_pairs={{0,8},{8,16},{16,24},{1,9},{9,17},{17,25},{2,10},{10,18},{18,26},{... | collective-permute-start | bytes 2312 | tf_op jit(solution)/shard_map/ppermute | solution.py:25
  24.0 5.7 %collective-permute-start.7 = (f32[3,1,1,8,128]{4,3,2,1,0:T(8,128)S(1)}, f32[3,1,1,8,128]{4,3,2,1,0:T(8,128)S(1)}, u32[]{:S(2)}, u32[]{:S(2)}) collective-permute-start(f32[3,1,1,8,128]{4,3,2,1,0:T(8,128)S(1)} %get-tuple-element.22), channel_id=1, source_target_pairs={{0,2},{2,4},{4,6},{6,0},{1,3},{3,5},{5,7},{7,1},{8,10},{10,12},{12... | collective-permute-start | bytes 36872 | tf_op jit(solution)/shard_map/ppermute | solution.py:16
  26.0 3.7 %collective-permute-start.6 = (f32[3,1,1,8,128]{4,3,2,1,0:T(8,128)S(1)}, f32[3,1,1,8,128]{4,3,2,1,0:T(8,128)S(1)}, u32[]{:S(2)}, u32[]{:S(2)}) collective-permute-start(f32[3,1,1,8,128]{4,3,2,1,0:T(8,128)S(1)} %get-tuple-element.23), channel_id=1, source_target_pairs={{2,0},{4,2},{6,4},{0,6},{3,1},{5,3},{7,5},{1,7},{10,8},{12,10},{14... | collective-permute-start | bytes 36872 | tf_op jit(solution)/shard_map/ppermute | solution.py:17
  27.1 5.6 %collective-permute-start.11 = (f32[3,1,8,8]{3,2,0,1:T(8,128)S(1)}, f32[3,1,8,8]{3,2,0,1:T(8,128)S(1)}, u32[]{:S(2)}, u32[]{:S(2)}) collective-permute-start(f32[3,1,8,8]{3,2,0,1:T(8,128)S(1)} %bitcast.51), channel_id=1, source_target_pairs={{8,0},{16,8},{24,16},{9,1},{17,9},{25,17},{10,2},{18,10},{26,18},{... | collective-permute-start | bytes 2312 | tf_op jit(solution)/shard_map/ppermute | solution.py:25
  29.8 3.1 %collective-permute-start.8 = (f32[3,1,10,1,128]{4,3,2,1,0:T(1,128)S(1)}, f32[3,1,10,1,128]{4,3,2,1,0:T(1,128)S(1)}, u32[]{:S(2)}, u32[]{:S(2)}) collective-permute-start(f32[3,1,10,1,128]{4,3,2,1,0:T(1,128)S(1)} %get-tuple-element.18), channel_id=1, source_target_pairs={{1,0},{0,1},{3,2},{2,3},{5,4},{4,5},{7,6},{6,7},{9,8},{8,9},{11,10... | collective-permute-start | bytes 46088 | tf_op jit(solution)/shard_map/ppermute | solution.py:17
  29.8 3.0 %collective-permute-start.9 = (f32[3,1,10,1,128]{4,3,2,1,0:T(1,128)S(1)}, f32[3,1,10,1,128]{4,3,2,1,0:T(1,128)S(1)}, u32[]{:S(2)}, u32[]{:S(2)}) collective-permute-start(f32[3,1,10,1,128]{4,3,2,1,0:T(1,128)S(1)} %get-tuple-element.19), channel_id=1, source_target_pairs={{0,1},{1,0},{2,3},{3,2},{4,5},{5,4},{6,7},{7,6},{8,9},{9,8},{10,11... | collective-permute-start | bytes 46088 | tf_op jit(solution)/shard_map/ppermute | solution.py:16
  30.4 2.5 %copy-start.4 = (bf16[2,3,1,8,8,128]{5,4,3,2,1,0:T(8,128)(2,1)S(1)}, bf16[2,3,1,8,8,128]{5,4,3,2,1,0:T(8,128)(2,1)}, u32[]{:S(2)}) copy-start(bf16[2,3,1,8,8,128]{5,4,3,2,1,0:T(8,128)(2,1)} %param.13) | copy-start | bytes 294916
where the time goes:
time: 35.5 us; the launch traced here: 35 us
  starting transfers between devices  18 us (51%)
  local copies, waits for them, and re-layouts  7.4 us (21%)
  waiting for transfers between devices  6.75 us (19%)
  between operations  1.54 us (4%)
  other arithmetic  1.3 us (4%)
    ppermute x4, starting transfers between devices, shifted(): return lax.ppermute(value, axis, pairs)  9.97 us
    ppermute x4, waiting for transfers between devices, shifted(): return lax.ppermute(value, axis, pairs)  6.68 us
    ppermute x4, starting transfers between devices, with_halo(): after = lax.ppermute(initial, axis, down)  5.06 us
    ppermute x4, starting transfers between devices, with_halo(): before = lax.ppermute(last, axis, up)  3.01 us
    unnamed x18, local copies, waits for them, and re-layouts  2.33 us
    gather x2, local copies, waits for them, and re-layouts, local(): jnp.take(from_above.reshape(3, rows * cols), flat_map, axis=1)  1.19 us
    reshape x2, local copies, waits for them, and re-layouts, local(): jnp.take(from_above.reshape(3, rows * cols), flat_map, axis=1)  1.05 us
    slice x1, local copies, waits for them, and re-layouts, local(): bottom = field[:, :, :, :, -1]  0.97 us
  transfers between devices with their start and end apart: 12, of which 4 were waited for; matrix products, arithmetic and copies ran while one was open for 13% of the time, Pallas kernels for 0%

commit v1 on v0

v1 whole, which is shorter than its diff:
```python
import functools

import jax
import jax.numpy as jnp
from jax import lax
from jax.experimental import pallas as pl
from jax.experimental.pallas import tpu as pltpu
from jax.sharding import PartitionSpec as P

MESH = pl.DeviceIdType.MESH
F32 = jnp.float32


def lane_roll(value, by):
    return pltpu.roll(value, by % value.shape[-1], value.ndim - 1)


def row_roll(value, by):
    return pltpu.roll(value, by % value.shape[-2], value.ndim - 2)


def kernel(
    grids, patches, u_hbm, w_hbm, k_hbm, s_hbm, f_hbm, m_hbm, i_hbm, out_ref, kern_ref,
    u_v, w_v, k_v, s_v, f_v, m_v, i_v, side_x, side_y, plane, got_x, got_y, got_z,
    load_sem, send_sem, recv_sem,
):
    g = lax.axis_index("grid")
    p = lax.axis_index("patch")
    q = lax.axis_index("cross")
    p_next = lax.rem(p + 1, patches)
    p_prev = lax.rem(p + patches - 1, patches)
    not_top = g > 0
    not_last = g < grids - 1

    barrier = pltpu.get_barrier_semaphore()
    pl.semaphore_signal(barrier, inc=1, device_id={"patch": p_next}, device_id_type=MESH)
    pl.semaphore_signal(barrier, inc=1, device_id={"patch": p_prev}, device_id_type=MESH)
    pl.semaphore_signal(barrier, inc=1, device_id={"cross": 1 - q}, device_id_type=MESH)

    @pl.when(not_top)
    def _():
        pl.semaphore_signal(barrier, inc=1, device_id={"grid": g - 1}, device_id_type=MESH)

    @pl.when(not_last)
    def _():
        pl.semaphore_signal(barrier, inc=1, device_id={"grid": g + 1}, device_id_type=MESH)

    pairs = ((u_hbm, u_v), (i_hbm, i_v), (m_hbm, m_v), (w_hbm, w_v), (k_hbm, k_v), (s_hbm, s_v), (f_hbm, f_v))
    loads = [pltpu.make_async_copy(a, b, load_sem.at[n]) for n, (a, b) in enumerate(pairs)]
    for load in loads:
        load.start()

    nc, nx, ny, nz = u_v.shape[0], u_v.shape[2], u_v.shape[3], u_v.shape[4]
    lane = lax.broadcasted_iota(jnp.int32, (ny, nz), 1)
    row = lax.broadcasted_iota(jnp.int32, (ny, nz), 0)
    odd = lax.rem(lane, 2) == 1

    @pl.when(jnp.logical_not(not_top))
    def _():
        got_z[:, 0] = jnp.zeros((2, ny, nz), F32)

    @pl.when(jnp.logical_not(not_last))
    def _():
        got_z[:, 1] = jnp.zeros((2, ny, nz), F32)

    def copies(step):
        def remote(src, dst, n, device):
            return pltpu.make_async_remote_copy(
                src_ref=src, dst_ref=dst, send_sem=send_sem.at[step, n], recv_sem=recv_sem.at[step, n],
                device_id=device, device_id_type=MESH,
            )

        return (
            remote(side_x.at[step, 1], got_x.at[step, 0], 0, {"patch": p_next}),
            remote(side_x.at[step, 0], got_x.at[step, 1], 1, {"patch": p_prev}),
            remote(side_y.at[step], got_y.at[step], 2, {"cross": 1 - q}),
            remote(plane.at[step], got_z.at[step, 0], 3, {"grid": g + 1}),
            remote(plane.at[step], got_z.at[step, 1], 4, {"grid": g - 1}),
        )

    def pack(step, u):
        side_x[step, 0] = u[:, 0]
        side_x[step, 1] = u[:, nx - 1]
        for c in range(nc):
            for x in range(nx):
                side_y[step, 0, c, x : x + 1] = u[c, x, ny - 1 : ny]
                side_y[step, 1, c, x : x + 1] = u[c, x, 0:1]
        packed = jnp.zeros((ny, nz), F32)
        for c in range(nc):
            for x in range(nx):
                k = c * nx + x
                packed = jnp.where(lax.div(lane, 2) == k, lane_roll(u[c, x], 2 * k + 1), packed)
        plane[step] = packed
        return packed

    def send(step):
        down, up = copies(step)[3:]

        @pl.when(not_last)
        def _():
            down.start()

        @pl.when(not_top)
        def _():
            up.start()

        for copy in copies(step)[:3]:
            copy.start()

    def receive(step):
        for copy in copies(step)[:3]:
            copy.wait_recv()
        down, up = copies(step)[3:]

        @pl.when(not_top)
        def _():
            down.wait_recv()

        @pl.when(not_last)
        def _():
            up.wait_recv()

    def finish(step):
        for copy in copies(step)[:3]:
            copy.wait_send()
        down, up = copies(step)[3:]

        @pl.when(not_last)
        def _():
            down.wait_send()

        @pl.when(not_top)
        def _():
            up.wait_send()

    def inner(u):
        none = jnp.zeros((nc, 1, ny, nz), F32)
        total = jnp.concatenate([u[:, 1:], none], axis=1) + jnp.concatenate([none, u[:, :-1]], axis=1)
        parts = []
        for c in range(nc):
            line = []
            for x in range(nx):
                cell = u[c, x]
                zs = jnp.where(lane == 0, 0.0, lane_roll(cell, 1)) + jnp.where(lane == nz - 1, 0.0, lane_roll(cell, -1))
                ys = jnp.where(row == 0, 0.0, row_roll(cell, 1)) + jnp.where(row == ny - 1, 0.0, row_roll(cell, -1))
                line.append(zs + ys)
            parts.append(jnp.stack(line))
        return total + jnp.stack(parts) - 6.0 * u

    def outer(step, packed, feeds):
        above = lane_roll(got_z[step, 0], 1)
        below = jnp.where(not_last, lane_roll(got_z[step, 1], -1), 0.0)
        fed = above
        for dx, dy, mask in feeds:
            moved = row_roll(above, -dy) if dy else above
            moved = lane_roll(moved, -2 * dx) if dx else moved
            fed = jnp.where(mask, moved, fed)
        ghost = jnp.where(odd, jnp.where(not_top, fed, packed), below)
        parts = []
        for c in range(nc):
            line = []
            for x in range(nx):
                k = c * nx + x
                zs = jnp.where((lane == 0) | (lane == nz - 1), lane_roll(ghost, -(2 * k + 1)), 0.0)
                first = jnp.broadcast_to(got_y[step, 0, c, x : x + 1], (ny, nz))
                last = jnp.broadcast_to(got_y[step, 1, c, x : x + 1], (ny, nz))
                ys = jnp.where(row == 0, first, jnp.where(row == ny - 1, last, 0.0))
                total = zs + ys
                if x == 0:
                    total = total + got_x[step, 0, c]
                if x == nx - 1:
                    total = total + got_x[step, 1, c]
                line.append(total)
            parts.append(jnp.stack(line))
        return jnp.stack(parts)

    loads[0].wait()
    u0 = u_v[:, 0]
    packed0 = pack(0, u0)
    pl.semaphore_wait(barrier, 3 + not_top.astype(jnp.int32) + not_last.astype(jnp.int32))
    send(0)

    loads[1].wait()
    own = i_v[0].astype(F32)
    spread = (lax.rem(lax.div(lax.broadcasted_iota(jnp.int32, (nz, nx), 0), 2), nx)
              == lax.broadcasted_iota(jnp.int32, (nz, nx), 1)).astype(F32)
    eye = (lax.broadcasted_iota(jnp.int32, (ny, ny), 0) == lax.broadcasted_iota(jnp.int32, (ny, ny), 1)).astype(F32)
    tall = jnp.dot(spread, own, preferred_element_type=F32)
    source = lax.dot_general(eye, tall, (((1,), (1,)), ((), ())), preferred_element_type=F32)
    here = lax.rem(lax.div(lane, 2), nx)
    feeds = []
    for dx in (-1, 0, 1):
        for dy in (-1, 0, 1):
            if dx or dy:
                feeds.append((dx, dy, source == ((here + dx) * ny + row + dy).astype(F32)))

    for load in loads[2:]:
        load.wait()
    mask = m_v[0, 0, 0].astype(F32)
    stiff = k_v[0] * mask
    base = (2.0 * u0 - w_v[:, 0] + s_v[1, :, 0].astype(F32)) * mask + stiff[None] * inner(u0)
    receive(0)
    u1 = base + stiff[None] * outer(0, packed0, feeds)
    packed1 = pack(1, u1)
    send(1)
    kern = jnp.sum(u1 * f_v[1, :, 0].astype(F32), axis=0)
    base = (2.0 * u1 - u0 + s_v[0, :, 0].astype(F32)) * mask + stiff[None] * inner(u1)
    receive(1)
    u2 = base + stiff[None] * outer(1, packed1, feeds)
    out_ref[:, 0] = u2
    kern_ref[0] = kern + jnp.sum(u2 * f_v[0, :, 0].astype(F32), axis=0)
    finish(0)
    finish(1)


def solution(mesh):
    grids, patches = mesh.shape["grid"], mesh.shape["patch"]

    def local(now, prev, stiffness, source, forward, mask, feed):
        nc, _, nx, ny, nz = now.shape
        args = (now, prev, stiffness, source, forward, mask, feed)
        vmem = [pltpu.VMEM(a.shape, a.dtype) for a in args]
        vmem[5] = pltpu.SMEM(mask.shape, mask.dtype)
        return pl.pallas_call(
            functools.partial(kernel, grids, patches),
            out_shape=(jax.ShapeDtypeStruct(now.shape, F32), jax.ShapeDtypeStruct(stiffness.shape, F32)),
            in_specs=[pl.BlockSpec(memory_space=pl.ANY)] * 7,
            out_specs=[pl.BlockSpec(memory_space=pltpu.VMEM)] * 2,
            scratch_shapes=vmem + [
                pltpu.VMEM((2, 2, nc, ny, nz), F32),
                pltpu.VMEM((2, 2, nc, nx, nz), F32),
                pltpu.VMEM((2, ny, nz), F32),
                pltpu.VMEM((2, 2, nc, ny, nz), F32),
                pltpu.VMEM((2, 2, nc, nx, nz), F32),
                pltpu.VMEM((2, 2, ny, nz), F32),
                pltpu.SemaphoreType.DMA((7,)),
                pltpu.SemaphoreType.DMA((2, 5)),
                pltpu.SemaphoreType.DMA((2, 5)),
            ],
            compiler_params=pltpu.CompilerParams(collective_id=0, has_side_effects=True),
        )(*args)

    in_specs = (
        P(None, "grid", "patch", "cross", None),
        P(None, "grid", "patch", "cross", None),
        P("grid", "patch", "cross", None),
        P(None, None, "grid", "patch", "cross", None),
        P(None, None, "grid", "patch", "cross", None),
        P("grid", "patch", "cross"),
        P("grid", "patch", "cross"),
    )
    out_specs = (P(None, "grid", "patch", "cross", None), P("grid", "patch", "cross", None))
    return jax.shard_map(local, mesh=mesh, in_specs=in_specs, out_specs=out_specs, check_vma=False)
```

time: 35.5 us -> 15.5 us (0.44)
  starting transfers between devices: 18 us -> 0 us
  Pallas kernels: 0 us -> 11.8 us
  waiting for transfers between devices: 6.75 us -> 0 us
  local copies, waits for them, and re-layouts: 7.4 us -> 2.16 us
  other arithmetic: 1.3 us -> 0 us
    ppermute x12 -> x0, starting transfers between devices: 18 us -> none  [the longest x4 9.97 us: shifted(): return lax.ppermute(value, axis, pairs)]
    pallas_call x0 -> x1, Pallas kernels: none -> 11.8 us  [local(): pl.pallas_call(functools.partial(kernel, grids, patches), out_shape=(jax....]
    ppermute x12 -> x0, waiting for transfers between devices: 6.75 us -> none  [the longest x4 6.68 us: shifted(): return lax.ppermute(value, axis, pairs)]
    slice x7 -> x0, local copies, waits for them, and re-layouts: 2.08 us -> none  [the longest x1 0.97 us: local(): bottom = field[:, :, :, :, -1]]
    gather x2 -> x0, local copies, waits for them, and re-layouts: 1.19 us -> none  [local(): jnp.take(from_above.reshape(3, rows * cols), flat_map, axis=1)]
    reshape x3 -> x0, local copies, waits for them, and re-layouts: 1.13 us -> none  [the longest x2 1.05 us: local(): jnp.take(from_above.reshape(3, rows * cols), flat_map, axis=1)]
    reduce_sum x1 -> x0, other arithmetic: 0.81 us -> none  [local(): jnp.sum(fresh * forward_field[slot].astype(jnp.float32), axis=0)]
    broadcast_in_dim x2 -> x0, local copies, waits for them, and re-layouts: 0.43 us -> none  [local(): lower = jnp.concatenate([field[..., 1:], from_below[..., None]], axis=4)]
  transfers between devices with their start and end apart: 12 -> 0, of which waited for: 4 -> 0; matrix products, arithmetic and copies ran while one was open for 13% -> 0% of each run, Pallas kernels for 0% -> 0%
where the time goes in v1:
time: 15.5 us; the launch traced here: 15.3 us
  Pallas kernels  11.8 us (76%)
  local copies, waits for them, and re-layouts  2.16 us (14%)
  between operations  1.29 us (8%)
    pallas_call x1, Pallas kernels, local(): pl.pallas_call(functools.partial(kernel, grids, patches), out_shape=(jax....  11.8 us
    unnamed x4, local copies, waits for them, and re-layouts  2.16 us

profile of v1, /device:TPU:0, one launch (start us, length us, event | category | flops | bytes accessed | tf_op | source)
XLA Modules:
  0.0 15.3 jit_solution(7291199896791830759)
XLA Ops:
  1.3 11.8 %shard_map.86 = (f32[3,1,8,8,128]{4,3,2,1,0:T(8,128)}, f32[1,8,8,128]{3,2,1,0:T(8,128)}) custom-call(f32[3,1,8,8,128]{4,3,2,1,0:T(8,128)} %u_hbm.1, f32[3,1,8,8,128]{4,3,2,1,0:T(8,128)} %w_hbm.1, f32[1,8,8,128]{3,2,1,0:T(8,128)} %k_hbm.1, bf16[2,3,1,8,8,128]{5,4,3,2,1,0:T(8,128)(2,1)} %s_hbm.1, bf16[2,3,1,8,8,128]{5,4,3,2,1,0:T(8,128)(2,1)} %f_hbm.1, ...), custom_call_target="tpu_custom_call" | custom-call | tf_op jit(solution)/shard_map/pallas_call | solution.py:224
  13.1 0.0 copy-start
  13.1 1.5 %copy.12 = f32[3,1,8,8,128]{4,3,2,1,0:T(8,128)} copy(f32[3,1,8,8,128]{4,3,2,1,0:T(8,128)} %get-tuple-element.4) | data formatting | bytes 196608
  14.7 0.0 copy-done
  14.7 0.6 %copy.13 = f32[1,8,8,128]{3,2,1,0:T(8,128)} copy(f32[1,8,8,128]{3,2,1,0:T(8,128)S(1)} %copy-done) | data formatting | bytes 65536
Async XLA Ops:
  13.1 1.6 %copy-start = (f32[1,8,8,128]{3,2,1,0:T(8,128)S(1)}, f32[1,8,8,128]{3,2,1,0:T(8,128)}, u32[]{:S(2)}) copy-start(f32[1,8,8,128]{3,2,1,0:T(8,128)} %get-tuple-element.5) | copy-start | bytes 98308

commit v2 on v1

--- a/solution.py
+++ b/solution.py
@@ -213,6 +213,15 @@
     finish(1)
 
 
+def store(field_ref, kern_ref, field_out, kern_out, sem):
+    first = pltpu.make_async_copy(field_ref, field_out, sem.at[0])
+    second = pltpu.make_async_copy(kern_ref, kern_out, sem.at[1])
+    first.start()
+    second.start()
+    first.wait()
+    second.wait()
+
+
 def solution(mesh):
     grids, patches = mesh.shape["grid"], mesh.shape["patch"]
 
@@ -221,10 +230,10 @@
         args = (now, prev, stiffness, source, forward, mask, feed)
         vmem = [pltpu.VMEM(a.shape, a.dtype) for a in args]
         vmem[5] = pltpu.SMEM(mask.shape, mask.dtype)
-        return pl.pallas_call(
+        done = pl.pallas_call(
             functools.partial(kernel, grids, patches),
-            out_shape=(jax.ShapeDtypeStruct(now.shape, F32), jax.ShapeDtypeStruct(stiffness.shape, F32)),
-            in_specs=[pl.BlockSpec(memory_space=pl.ANY)] * 7,
+            out_shape=(pltpu.VMEM(now.shape, F32), pltpu.VMEM(stiffness.shape, F32)),
+            in_specs=[pl.BlockSpec(memory_space=pltpu.HBM)] * 7,
             out_specs=[pl.BlockSpec(memory_space=pltpu.VMEM)] * 2,
             scratch_shapes=vmem + [
                 pltpu.VMEM((2, 2, nc, ny, nz), F32),
@@ -239,6 +248,13 @@
             ],
             compiler_params=pltpu.CompilerParams(collective_id=0, has_side_effects=True),
         )(*args)
+        return pl.pallas_call(
+            store,
+            out_shape=(pltpu.HBM(now.shape, F32), pltpu.HBM(stiffness.shape, F32)),
+            in_specs=[pl.BlockSpec(memory_space=pl.ANY)] * 2,
+            out_specs=[pl.BlockSpec(memory_space=pltpu.HBM)] * 2,
+            scratch_shapes=[pltpu.SemaphoreType.DMA((2,))],
+        )(*[pltpu.with_memory_space_constraint(d, pltpu.VMEM) for d in done])
 
     in_specs = (
         P(None, "grid", "patch", "cross", None),

time: 15.5 us -> 13.3 us (0.86)
  local copies, waits for them, and re-layouts: 2.16 us -> 0 us
    unnamed x4 -> x0, local copies, waits for them, and re-layouts: 2.16 us -> none
    pallas_call x1 -> x2, Pallas kernels: 11.8 us -> 11.9 us  [the longest x1 11.2 us: local(): pl.pallas_call(functools.partial(kernel, grids, patches), out_shape=(pltp...]
where the time goes in v2:
time: 13.3 us; the launch traced here: 13.2 us
  Pallas kernels  11.9 us (89%)
  between operations  1.29 us (10%)
    pallas_call x1, Pallas kernels, local(): pl.pallas_call(functools.partial(kernel, grids, patches), out_shape=(pltp...  11.2 us
    pallas_call x1, Pallas kernels, local(): pl.pallas_call(store, out_shape=(pltpu.HBM(now.shape, F32), pltpu.HBM(sti...  0.67 us

profile of v2, /device:TPU:0, one launch (start us, length us, event | category | flops | bytes accessed | tf_op | source)
XLA Modules:
  0.0 13.2 jit_solution(15354531291647150881)
XLA Ops:
  1.3 11.2 %shard_map.86 = (f32[3,1,8,8,128]{4,3,2,1,0:T(8,128)S(1)}, f32[1,8,8,128]{3,2,1,0:T(8,128)S(1)}) custom-call(f32[3,1,8,8,128]{4,3,2,1,0:T(8,128)} %u_hbm.1, f32[3,1,8,8,128]{4,3,2,1,0:T(8,128)} %w_hbm.1, f32[1,8,8,128]{3,2,1,0:T(8,128)} %k_hbm.1, bf16[2,3,1,8,8,128]{5,4,3,2,1,0:T(8,128)(2,1)} %s_hbm.1, bf16[2,3,1,8,8,128]{5,4,3,2,1,0:T(8,128)(2,1)} %f_hbm.1, ...), custom_call_target="tpu_custom_call" | custom-call | tf_op jit(solution)/shard_map/pallas_call | solution.py:233
  12.5 0.7 %shard_map.87 = (f32[3,1,8,8,128]{4,3,2,1,0:T(8,128)}, f32[1,8,8,128]{3,2,1,0:T(8,128)}) custom-call(f32[3,1,8,8,128]{4,3,2,1,0:T(8,128)S(1)} %get-tuple-element.4.field_ref, f32[1,8,8,128]{3,2,1,0:T(8,128)S(1)} %get-tuple-element.5.kern_ref), custom_call_target="tpu_custom_call" | custom-call | tf_op jit(solution)/shard_map/pallas_call | solution.py:251

commit v3 on v2

v3 whole, which is shorter than its diff:
```python
import functools

import jax
import jax.numpy as jnp
from jax import lax
from jax.experimental import pallas as pl
from jax.experimental.pallas import tpu as pltpu
from jax.sharding import PartitionSpec as P

MESH = pl.DeviceIdType.MESH
F32 = jnp.float32


def lane_roll(value, by):
    return pltpu.roll(value, by % value.shape[-1], value.ndim - 1)


def row_roll(value, by):
    return pltpu.roll(value, by % value.shape[-2], value.ndim - 2)


def kernel(
    grids, patches, u_hbm, w_hbm, k_hbm, s_hbm, f_hbm, m_ref, i_hbm, out_ref, kern_ref,
    u_v, w_v, k_v, s_v, f_v, i_v, side_y, out_p, out_g, out_c, got_y, got_p, got_g, got_d, got_q, got_c,
    load_sem, send_sem, recv_sem,
):
    g = lax.axis_index("grid")
    p = lax.axis_index("patch")
    q = lax.axis_index("cross")
    nxt = lax.rem(p + 1, patches)
    prv = lax.rem(p + patches - 1, patches)
    far = 1 - q
    not_top = g > 0
    not_last = g < grids - 1

    flat = (
        (out_p.at[1], got_p.at[0], (g, nxt, q)),
        (out_p.at[0], got_p.at[1], (g, prv, q)),
        (out_c.at[1], got_c.at[0], (g, nxt, far)),
        (out_c.at[0], got_c.at[1], (g, prv, far)),
        (side_y.at[0], got_y.at[0], (g, p, far)),
        (side_y.at[1], got_y.at[1], (g, p, far)),
    )

    def vertical(slot, other):
        return (
            (out_g, got_g.at[slot], (other, p, q)),
            (out_g.at[0], got_d.at[0, slot], (other, nxt, q)),
            (out_g.at[0], got_d.at[1, slot], (other, prv, q)),
            (out_g.at[0], got_q.at[slot], (other, p, far)),
        )

    down, up = vertical(0, g + 1), vertical(1, g - 1)

    def run(messages, first, what):
        for n, (src, dst, device) in enumerate(messages):
            copy = pltpu.make_async_remote_copy(
                src_ref=src, dst_ref=dst, send_sem=send_sem.at[first + n], recv_sem=recv_sem.at[first + n],
                device_id=device, device_id_type=MESH,
            )
            getattr(copy, what)()

    barrier = pltpu.get_barrier_semaphore()

    def greet(messages):
        for _, _, device in messages:
            pl.semaphore_signal(barrier, inc=1, device_id=device, device_id_type=MESH)

    def both(condition, body):
        @pl.when(condition)
        def _():
            body()

    greet(flat[:5])
    both(not_last, lambda: greet(down))
    both(not_top, lambda: greet(up))

    pairs = ((u_hbm, u_v), (w_hbm, w_v), (k_hbm, k_v), (s_hbm, s_v), (i_hbm, i_v), (f_hbm, f_v))
    loads = [pltpu.make_async_copy(a, b, load_sem.at[n]) for n, (a, b) in enumerate(pairs)]
    for load in loads:
        load.start()

    nc, nx, ny, nz = u_v.shape[0], u_v.shape[2], u_v.shape[3], u_v.shape[4]
    lane = lax.broadcasted_iota(jnp.int32, (ny, nz), 1)
    row = lax.broadcasted_iota(jnp.int32, (ny, nz), 0)
    here = lax.rem(lax.div(lane, 2), nx)
    odd = lax.rem(lane, 2) == 1

    def clear(slot):
        got_g[slot] = jnp.zeros((4, ny, nz), F32)
        got_d[:, slot] = jnp.zeros((2, ny, nz), F32)
        got_q[slot] = jnp.zeros((ny, nz), F32)

    both(jnp.logical_not(not_top), lambda: clear(0))
    both(jnp.logical_not(not_last), lambda: clear(1))

    def pack(cells):
        packed = jnp.zeros((ny, nz), F32)
        for k, cell in enumerate(cells):
            packed = jnp.where(lax.div(lane, 2) == k, lane_roll(cell, 2 * k + 1), packed)
        return packed

    def sides(step, u):
        for c in range(nc):
            for x in range(nx):
                side_y[step, 0, c, x : x + 1] = u[c, x, ny - 1 : ny]
                side_y[step, 1, c, x : x + 1] = u[c, x, 0:1]

    def inner(u):
        none = jnp.zeros((nc, 1, ny, nz), F32)
        total = jnp.concatenate([u[:, 1:], none], axis=1) + jnp.concatenate([none, u[:, :-1]], axis=1)
        parts = []
        for c in range(nc):
            line = []
            for x in range(nx):
                cell = u[c, x]
                zs = jnp.where(lane == 0, 0.0, lane_roll(cell, 1)) + jnp.where(lane == nz - 1, 0.0, lane_roll(cell, -1))
                ys = jnp.where(row == 0, 0.0, row_roll(cell, 1)) + jnp.where(row == ny - 1, 0.0, row_roll(cell, -1))
                line.append(zs + ys)
            parts.append(jnp.stack(line))
        return total + jnp.stack(parts) - 6.0 * u

    def feeds(source):
        found = []
        for dx in (-1, 0, 1):
            for dy in (-1, 0, 1):
                if dx or dy:
                    found.append((dx, dy, source == ((here + dx) * ny + row + dy).astype(F32)))
        return found

    def fed_by(bottoms, masks):
        above = lane_roll(bottoms, 1)
        fed = above
        for dx, dy, mask in masks:
            moved = row_roll(above, -dy) if dy else above
            moved = lane_roll(moved, -2 * dx) if dx else moved
            fed = jnp.where(mask, moved, fed)
        return fed

    def ghost_tile(above, below, masks):
        return jnp.where(odd, fed_by(above, masks), lane_roll(below, -1))

    def ends(ghost, k, cell):
        moved = lane_roll(ghost, -(2 * k + 1))
        first = jnp.where(not_top, moved, cell)
        return jnp.where(lane == 0, first, jnp.where(lane == nz - 1, moved, 0.0))

    def rims(first, last):
        first = jnp.broadcast_to(first, (ny, nz))
        last = jnp.broadcast_to(last, (ny, nz))
        return jnp.where(row == 0, first, jnp.where(row == ny - 1, last, 0.0))

    def outer(step, u, ghost, before, after):
        parts = []
        for c in range(nc):
            line = []
            for x in range(nx):
                total = ends(ghost, c * nx + x, u[c, x])
                total = total + rims(got_y[step, 0, c, x : x + 1], got_y[step, 1, c, x : x + 1])
                if x == 0:
                    total = total + before[c]
                if x == nx - 1:
                    total = total + after[c]
                line.append(total)
            parts.append(jnp.stack(line))
        return jnp.stack(parts)

    loads[0].wait()
    u0 = u_v[:, 0]
    sides(0, u0)
    for e, x in ((0, 0), (1, nx - 1)):
        out_p[e, 0:nc] = u0[:, x]
        for c in range(nc):
            out_c[e, c : c + 1] = u0[c, x, ny - 1 : ny]
            out_c[e, nc + c : nc + c + 1] = u0[c, x, 0:1]
        out_c[e, 2 * nc :] = jnp.zeros((ny - 2 * nc, nz), F32)
    packed = pack([u0[c, x] for c in range(nc) for x in range(nx)])
    out_g[0] = packed
    for load in loads[1:5]:
        load.wait()
    mask = m_ref[0, 0, 0].astype(F32)
    stiff = k_v[0] * mask
    base = (2.0 * u0 - w_v[:, 0] + s_v[1, :, 0].astype(F32)) * mask + stiff[None] * inner(u0)
    own = i_v[0].astype(F32)
    spread = (lax.rem(lax.div(lax.broadcasted_iota(jnp.int32, (nz, nx), 0), 2), nx)
              == lax.broadcasted_iota(jnp.int32, (nz, nx), 1)).astype(F32)
    eye = (lax.broadcasted_iota(jnp.int32, (ny, ny), 0) == lax.broadcasted_iota(jnp.int32, (ny, ny), 1)).astype(F32)
    tall = jnp.dot(spread, own, preferred_element_type=F32)
    source = lax.dot_general(eye, tall, (((1,), (1,)), ((), ())), preferred_element_type=F32)
    for e, x in ((0, 0), (1, nx - 1)):
        out_p[e, nc : 2 * nc] = base[:, x]
        out_p[e, 2 * nc] = stiff[x]
        out_p[e, 2 * nc + 1] = source
    out_g[1] = pack([base[c, x] for c in range(nc) for x in range(nx)])
    out_g[2] = pack([stiff[x] for c in range(nc) for x in range(nx)])
    out_g[3] = source

    vertical_count = len(down)
    pl.semaphore_wait(barrier, 5 + vertical_count * (not_top.astype(jnp.int32) + not_last.astype(jnp.int32)))
    both(not_last, lambda: run(down, 6, "start"))
    both(not_top, lambda: run(up, 10, "start"))
    run(flat[:5], 0, "start")
    loads[5].wait()
    masks = feeds(source)
    run(flat[:5], 0, "wait_recv")
    both(not_top, lambda: run(down, 6, "wait_recv"))
    both(not_last, lambda: run(up, 10, "wait_recv"))

    ghost = ghost_tile(got_g[0, 0], got_g[1, 0], masks)
    u1 = base + stiff[None] * outer(0, u0, ghost, got_p[0, 0:nc], got_p[1, 0:nc])
    sides(1, u1)
    run(flat[5:], 5, "start")

    planes = []
    for e, x, beside in ((0, nx - 1, 0), (1, 0, nx - 1)):
        near = ghost_tile(got_d[e, 0], got_d[e, 1], feeds(got_p[e, 2 * nc + 1]))
        plane = []
        for c in range(nc):
            total = ends(near, c * nx + x, got_p[e, c]) + u0[c, beside]
            total = total + rims(got_c[e, c : c + 1], got_c[e, nc + c : nc + c + 1])
            plane.append(got_p[e, nc + c] + got_p[e, 2 * nc] * total)
        planes.append(plane)

    tiles = []
    for slot in range(2):
        if slot == 0:
            total = lane_roll(packed, -1)
        else:
            total = fed_by(packed, feeds(got_g[1, 3]))
        total = total + jnp.where(here == 0, lane_roll(got_d[0, slot], -2 * (nx - 1)), 0.0)
        total = total + jnp.where(here == nx - 1, lane_roll(got_d[1, slot], 2 * (nx - 1)), 0.0)
        total = total + jnp.where(row == 0, row_roll(got_q[slot], 1), 0.0)
        total = total + jnp.where(row == ny - 1, row_roll(got_q[slot], -1), 0.0)
        tiles.append(got_g[slot, 1] + got_g[slot, 2] * total)
    ghost = ghost_tile(tiles[0], tiles[1], masks)

    kern = jnp.sum(u1 * f_v[1, :, 0].astype(F32), axis=0)
    base = (2.0 * u1 - u0 + s_v[0, :, 0].astype(F32)) * mask + stiff[None] * inner(u1)
    run(flat[5:], 5, "wait_recv")
    u2 = base + stiff[None] * outer(1, u1, ghost, planes[0], planes[1])
    out_ref[:, 0] = u2
    kern_ref[0] = kern + jnp.sum(u2 * f_v[0, :, 0].astype(F32), axis=0)
    run(flat, 0, "wait_send")
    both(not_last, lambda: run(down, 6, "wait_send"))
    both(not_top, lambda: run(up, 10, "wait_send"))


def store(field_ref, kern_ref, field_out, kern_out, sem):
    first = pltpu.make_async_copy(field_ref, field_out, sem.at[0])
    second = pltpu.make_async_copy(kern_ref, kern_out, sem.at[1])
    first.start()
    second.start()
    first.wait()
    second.wait()


def solution(mesh):
    grids, patches = mesh.shape["grid"], mesh.shape["patch"]

    def local(now, prev, stiffness, source, forward, mask, feed):
        nc, _, nx, ny, nz = now.shape
        args = (now, prev, stiffness, source, forward, mask, feed)
        vmem = [pltpu.VMEM(a.shape, a.dtype) for a in args if a is not mask]
        tile = (ny, nz)
        return_shapes = (pltpu.VMEM(now.shape, F32), pltpu.VMEM(stiffness.shape, F32))
        done = pl.pallas_call(
            functools.partial(kernel, grids, patches),
            out_shape=return_shapes,
            in_specs=[pl.BlockSpec(memory_space=pltpu.HBM)] * 5
            + [pl.BlockSpec(memory_space=pltpu.SMEM), pl.BlockSpec(memory_space=pltpu.HBM)],
            out_specs=[pl.BlockSpec(memory_space=pltpu.VMEM)] * 2,
            scratch_shapes=vmem + [
                pltpu.VMEM((2, 2, nc, nx, nz), F32),
                pltpu.VMEM((2, 2 * nc + 2) + tile, F32),
                pltpu.VMEM((4,) + tile, F32),
                pltpu.VMEM((2,) + tile, F32),
                pltpu.VMEM((2, 2, nc, nx, nz), F32),
                pltpu.VMEM((2, 2 * nc + 2) + tile, F32),
                pltpu.VMEM((2, 4) + tile, F32),
                pltpu.VMEM((2, 2) + tile, F32),
                pltpu.VMEM((2,) + tile, F32),
                pltpu.VMEM((2,) + tile, F32),
                pltpu.SemaphoreType.DMA((6,)),
                pltpu.SemaphoreType.DMA((14,)),
                pltpu.SemaphoreType.DMA((14,)),
            ],
            compiler_params=pltpu.CompilerParams(collective_id=0, has_side_effects=True),
        )(*args)
        return pl.pallas_call(
            store,
            out_shape=(pltpu.HBM(now.shape, F32), pltpu.HBM(stiffness.shape, F32)),
            in_specs=[pl.BlockSpec(memory_space=pl.ANY)] * 2,
            out_specs=[pl.BlockSpec(memory_space=pltpu.HBM)] * 2,
            scratch_shapes=[pltpu.SemaphoreType.DMA((2,))],
        )(*[pltpu.with_memory_space_constraint(d, pltpu.VMEM) for d in done])

    in_specs = (
        P(None, "grid", "patch", "cross", None),
        P(None, "grid", "patch", "cross", None),
        P("grid", "patch", "cross", None),
        P(None, None, "grid", "patch", "cross", None),
        P(None, None, "grid", "patch", "cross", None),
        P("grid", "patch", "cross"),
        P("grid", "patch", "cross"),
    )
    out_specs = (P(None, "grid", "patch", "cross", None), P("grid", "patch", "cross", None))
    return jax.shard_map(local, mesh=mesh, in_specs=in_specs, out_specs=out_specs, check_vma=False)
```

time: 13.3 us -> 11.9 us (0.89)
  Pallas kernels: 11.9 us -> 10.5 us
    pallas_call x1, Pallas kernels: 11.2 us -> 9.79 us  [local(): pl.pallas_call(functools.partial(kernel, grids, patches), out_shape=retur...]
where the time goes in v3:
time: 11.9 us; the launch traced here: 11.7 us
  Pallas kernels  10.5 us (88%)
  between operations  1.29 us (11%)
    pallas_call x1, Pallas kernels, local(): pl.pallas_call(functools.partial(kernel, grids, patches), out_shape=retur...  9.79 us
    pallas_call x1, Pallas kernels, local(): pl.pallas_call(store, out_shape=(pltpu.HBM(now.shape, F32), pltpu.HBM(sti...  0.67 us

profile of v3, /device:TPU:0, one launch (start us, length us, event | category | flops | bytes accessed | tf_op | source)
XLA Modules:
  0.0 11.7 jit_solution(5730676302295427016)
XLA Ops:
  1.3 9.8 %shard_map.86 = (f32[3,1,8,8,128]{4,3,2,1,0:T(8,128)S(1)}, f32[1,8,8,128]{3,2,1,0:T(8,128)S(1)}) custom-call(f32[3,1,8,8,128]{4,3,2,1,0:T(8,128)} %u_hbm.1, f32[3,1,8,8,128]{4,3,2,1,0:T(8,128)} %w_hbm.1, f32[1,8,8,128]{3,2,1,0:T(8,128)} %k_hbm.1, bf16[2,3,1,8,8,128]{5,4,3,2,1,0:T(8,128)(2,1)} %s_hbm.1, bf16[2,3,1,8,8,128]{5,4,3,2,1,0:T(8,128)(2,1)} %f_hbm.1, ...), custom_call_target="tpu_custom_call" | custom-call | tf_op jit(solution)/shard_map/pallas_call | solution.py:266
  11.1 0.7 %shard_map.87 = (f32[3,1,8,8,128]{4,3,2,1,0:T(8,128)}, f32[1,8,8,128]{3,2,1,0:T(8,128)}) custom-call(f32[3,1,8,8,128]{4,3,2,1,0:T(8,128)S(1)} %get-tuple-element.4.field_ref, f32[1,8,8,128]{3,2,1,0:T(8,128)S(1)} %get-tuple-element.5.kern_ref), custom_call_target="tpu_custom_call" | custom-call | tf_op jit(solution)/shard_map/pallas_call | solution.py:289

commit v4 on v3

--- a/solution.py
+++ b/solution.py
@@ -21,7 +21,7 @@
 
 def kernel(
     grids, patches, u_hbm, w_hbm, k_hbm, s_hbm, f_hbm, m_ref, i_hbm, out_ref, kern_ref,
-    u_v, w_v, k_v, s_v, f_v, i_v, side_y, out_p, out_g, out_c, got_y, got_p, got_g, got_d, got_q, got_c,
+    u_v, i_v, k_v, w_v, s_v, f_v, side_y, out_p, out_g, out_c, got_y, got_p, got_g, got_d, got_q, got_c,
     load_sem, send_sem, recv_sem,
 ):
     g = lax.axis_index("grid")
@@ -71,14 +71,14 @@
         def _():
             body()
 
+    pairs = ((u_hbm, u_v), (i_hbm, i_v), (k_hbm, k_v), (w_hbm, w_v), (s_hbm, s_v), (f_hbm, f_v))
+    loads = [pltpu.make_async_copy(a, b, load_sem.at[n]) for n, (a, b) in enumerate(pairs)]
+    for load in loads:
+        load.start()
+
     greet(flat[:5])
     both(not_last, lambda: greet(down))
     both(not_top, lambda: greet(up))
-
-    pairs = ((u_hbm, u_v), (w_hbm, w_v), (k_hbm, k_v), (s_hbm, s_v), (i_hbm, i_v), (f_hbm, f_v))
-    loads = [pltpu.make_async_copy(a, b, load_sem.at[n]) for n, (a, b) in enumerate(pairs)]
-    for load in loads:
-        load.start()
 
     nc, nx, ny, nz = u_v.shape[0], u_v.shape[2], u_v.shape[3], u_v.shape[4]
     lane = lax.broadcasted_iota(jnp.int32, (ny, nz), 1)
@@ -176,24 +176,28 @@
         out_c[e, 2 * nc :] = jnp.zeros((ny - 2 * nc, nz), F32)
     packed = pack([u0[c, x] for c in range(nc) for x in range(nx)])
     out_g[0] = packed
-    for load in loads[1:5]:
-        load.wait()
-    mask = m_ref[0, 0, 0].astype(F32)
-    stiff = k_v[0] * mask
-    base = (2.0 * u0 - w_v[:, 0] + s_v[1, :, 0].astype(F32)) * mask + stiff[None] * inner(u0)
+    loads[1].wait()
     own = i_v[0].astype(F32)
     spread = (lax.rem(lax.div(lax.broadcasted_iota(jnp.int32, (nz, nx), 0), 2), nx)
               == lax.broadcasted_iota(jnp.int32, (nz, nx), 1)).astype(F32)
     eye = (lax.broadcasted_iota(jnp.int32, (ny, ny), 0) == lax.broadcasted_iota(jnp.int32, (ny, ny), 1)).astype(F32)
     tall = jnp.dot(spread, own, preferred_element_type=F32)
     source = lax.dot_general(eye, tall, (((1,), (1,)), ((), ())), preferred_element_type=F32)
+    out_g[3] = source
+    loads[2].wait()
+    mask = m_ref[0, 0, 0].astype(F32)
+    stiff = k_v[0] * mask
+    third = pack([stiff[x] for x in range(nx)])
+    out_g[2] = third + lane_roll(third, 2 * nx) + lane_roll(third, 4 * nx)
+    rest = stiff[None] * inner(u0)
+    loads[3].wait()
+    loads[4].wait()
+    base = (2.0 * u0 - w_v[:, 0] + s_v[1, :, 0].astype(F32)) * mask + rest
     for e, x in ((0, 0), (1, nx - 1)):
         out_p[e, nc : 2 * nc] = base[:, x]
         out_p[e, 2 * nc] = stiff[x]
         out_p[e, 2 * nc + 1] = source
     out_g[1] = pack([base[c, x] for c in range(nc) for x in range(nx)])
-    out_g[2] = pack([stiff[x] for c in range(nc) for x in range(nx)])
-    out_g[3] = source
 
     vertical_count = len(down)
     pl.semaphore_wait(barrier, 5 + vertical_count * (not_top.astype(jnp.int32) + not_last.astype(jnp.int32)))
@@ -261,6 +265,7 @@
         nc, _, nx, ny, nz = now.shape
         args = (now, prev, stiffness, source, forward, mask, feed)
         vmem = [pltpu.VMEM(a.shape, a.dtype) for a in args if a is not mask]
+        vmem = [vmem[n] for n in (0, 5, 2, 1, 3, 4)]
         tile = (ny, nz)
         return_shapes = (pltpu.VMEM(now.shape, F32), pltpu.VMEM(stiffness.shape, F32))
         done = pl.pallas_call(

time: 11.9 us -> 11.9 us (level)
  no operation moved by 1% of the time
where the time goes in v4:
time: 11.9 us; the launch traced here: 11.7 us
  Pallas kernels  10.5 us (88%)
  between operations  1.29 us (11%)
    pallas_call x1, Pallas kernels, local(): pl.pallas_call(functools.partial(kernel, grids, patches), out_shape=retur...  9.79 us
    pallas_call x1, Pallas kernels, local(): pl.pallas_call(store, out_shape=(pltpu.HBM(now.shape, F32), pltpu.HBM(sti...  0.67 us

profile of v4, /device:TPU:0, one launch (start us, length us, event | category | flops | bytes accessed | tf_op | source)
XLA Modules:
  0.0 11.7 jit_solution(13299902860912673238)
XLA Ops:
  1.3 9.8 %shard_map.86 = (f32[3,1,8,8,128]{4,3,2,1,0:T(8,128)S(1)}, f32[1,8,8,128]{3,2,1,0:T(8,128)S(1)}) custom-call(f32[3,1,8,8,128]{4,3,2,1,0:T(8,128)} %u_hbm.1, f32[3,1,8,8,128]{4,3,2,1,0:T(8,128)} %w_hbm.1, f32[1,8,8,128]{3,2,1,0:T(8,128)} %k_hbm.1, bf16[2,3,1,8,8,128]{5,4,3,2,1,0:T(8,128)(2,1)} %s_hbm.1, bf16[2,3,1,8,8,128]{5,4,3,2,1,0:T(8,128)(2,1)} %f_hbm.1, ...), custom_call_target="tpu_custom_call" | custom-call | tf_op jit(solution)/shard_map/pallas_call | solution.py:271
  11.1 0.7 %shard_map.87 = (f32[3,1,8,8,128]{4,3,2,1,0:T(8,128)}, f32[1,8,8,128]{3,2,1,0:T(8,128)}) custom-call(f32[3,1,8,8,128]{4,3,2,1,0:T(8,128)S(1)} %get-tuple-element.4.field_ref, f32[1,8,8,128]{3,2,1,0:T(8,128)S(1)} %get-tuple-element.5.kern_ref), custom_call_target="tpu_custom_call" | custom-call | tf_op jit(solution)/shard_map/pallas_call | solution.py:294
